TPU v7x, 32 devices: a whole 2x2x4 slice. The times are simulated.
32 devices in a mesh: tile: 8 (over y, x, core), wave: 4 (over z).
Axes of the slice: x: 2, y: 2, z: 4, core: 2. Of those that a mesh axis runs over, the one named last changes fastest.
Arguments:
- maps: float32 [4, 128, 1024], P(None, None, 'tile'), may hold values from 0 to 2
- measured: float32 [16, 128, 128], P('tile'), may hold values from 0 to 8
- offsets: int32 [16], P('tile'), may hold values from -64 to 64, as said below
- probe: float32 [48, 2, 128, 128], P('wave'), may hold values from -6 to 6
- spectrum: float32 [48], P('wave'), may hold values from 0.05 to 0.5
- wave_index: int32 [48], P('wave'), may hold values from 0 to 47, each once
- edge_band: int32 [48, 4], P('wave'), may hold values from 0 to 2
- band_coef: float32 [2, 3, 4], replicated, may hold values from 0.1 to 0.8
Outputs:
- new_maps: float32 [4, 128, 1024], P(None, None, 'tile')
Inputs may be any that keep to these rules, and one draw needn't show every extreme that they name: `offsets`: a frame reaches at most 64 columns into either neighbouring tile; in every tile one frame starts exactly 64 columns before the tile and another ends exactly 64 columns after it. `wave_index`: each wavelength is held by exactly one slot.
All inputs are finite; a program needn't handle non-finite values.
Results may differ from a plain program's by a relative error of at most 0.0024.
Values sent between devices are 32-bit elements; how exact they have to be, the bound alone decides.
No kernel may reach another device: no remote copies, remote signals or barrier semaphores. Data moves between devices by JAX's collectives and lax.ppermute only.
A program may use at most 64 MiB of HBM per device.

v0:
```python
import math
import jax
import jax.numpy as jnp
from jax import lax
from jax.sharding import PartitionSpec as P

WAVES = 48
relax = 4.0
floor_level = 1.0


def padded(block, sides, width):
    for axis, dim in sides:
        count = lax.axis_size(axis)
        forward = [(i, i + 1) for i in range(count - 1)]
        backward = [(target, source) for source, target in forward]
        low = lax.ppermute(
            lax.slice_in_dim(block, block.shape[dim] - width, None, axis=dim), axis, forward
        )
        high = lax.ppermute(lax.slice_in_dim(block, 0, width, axis=dim), axis, backward)
        block = jnp.concatenate([low, block, high], axis=dim)
    return block


def chirp_table(which_wave, length):
    centred = jnp.arange(length, dtype=jnp.int32) - length // 2
    product = (centred[:, None] * centred[None, :]).astype(jnp.float32)
    sampling = 0.6 + 0.4 * which_wave.astype(jnp.float32) / (WAVES - 1)
    phase_angle = -2.0 * math.pi / length * sampling[..., None, None] * product
    normaliser = 1.0 / math.sqrt(length)
    return (
        (jnp.cos(phase_angle) * normaliser).astype(jnp.bfloat16),
        (jnp.sin(phase_angle) * normaliser).astype(jnp.bfloat16),
    )


def left_product(table, data):
    return jnp.einsum("kn,fnj->fkj", table, data, preferred_element_type=jnp.float32)


def right_product(data, table):
    return jnp.einsum("fkn,nj->fkj", data, table, preferred_element_type=jnp.float32)


def transform(table_re, table_im, data_re, data_im):
    mid_re = (left_product(table_re, data_re) - left_product(table_im, data_im)).astype(
        jnp.bfloat16
    )
    mid_im = (left_product(table_re, data_im) + left_product(table_im, data_re)).astype(
        jnp.bfloat16
    )
    out_re = right_product(mid_re, table_re) - right_product(mid_im, table_im)
    out_im = right_product(mid_re, table_im) + right_product(mid_im, table_re)
    return (out_re, out_im)


def fold_rims(interior, arrived, margin):
    columns = interior.shape[2]
    left_part = interior[:, :, :margin] + arrived[:, :, :margin]
    middle = interior[:, :, margin : columns - margin]
    right_part = interior[:, :, columns - margin :] + arrived[:, :, arrived.shape[2] - margin :]
    return jnp.concatenate([left_part, middle, right_part], axis=2)


def edge_cells(accumulated, margin):
    width = accumulated.shape[2]
    return jnp.concatenate(
        [accumulated[:, :, :margin], accumulated[:, :, width - margin :]], axis=2
    )


def place_frames(stacked, offsets, columns, margin):
    frame_count, channels, length = (stacked.shape[0], stacked.shape[1], stacked.shape[2])
    accumulated = jnp.zeros((channels, length, columns + 2 * margin), jnp.float32)
    for frame in range(frame_count):
        current = lax.dynamic_slice_in_dim(accumulated, offsets[frame] + margin, length, 2)
        accumulated = lax.dynamic_update_slice_in_dim(
            accumulated, current + stacked[frame], offsets[frame] + margin, 2
        )
    return accumulated


def per_device(maps, measured, offsets, probe, spectrum, wave_index, edge_band, band_coef):
    materials, length, columns = maps.shape
    frame_count = measured.shape[0]
    band_count = band_coef.shape[1]
    margin = length // 2
    extended = padded(maps, (("tile", 2),), margin)
    windows = jnp.stack(
        [
            lax.dynamic_slice_in_dim(extended, offsets[frame] + margin, length, 2)
            for frame in range(frame_count)
        ]
    )
    onehot = (edge_band[:, :, None] == jnp.arange(band_count, dtype=jnp.int32)).astype(jnp.float32)
    coefficient = jnp.einsum("smb,cbm->csm", onehot, band_coef, precision=lax.Precision.HIGHEST)

    def forward_slot(partial_value, inputs):
        wave_probe, absorb_coef, phase_coef, weight, which_wave = inputs
        absorb = jnp.einsum("m,fmrk->frk", absorb_coef, windows, precision=lax.Precision.HIGHEST)
        phase_sum = jnp.einsum("m,fmrk->frk", phase_coef, windows, precision=lax.Precision.HIGHEST)
        damping = jnp.exp(-absorb)
        obj_re = damping * jnp.cos(phase_sum)
        obj_im = damping * jnp.sin(phase_sum)
        psi_re = wave_probe[0] * obj_re - wave_probe[1] * obj_im
        psi_im = wave_probe[0] * obj_im + wave_probe[1] * obj_re
        table_re, table_im = chirp_table(which_wave, length)
        far_re, far_im = transform(
            table_re, table_im, psi_re.astype(jnp.bfloat16), psi_im.astype(jnp.bfloat16)
        )
        partial_value = partial_value + weight * (far_re * far_re + far_im * far_im)
        return (partial_value, (table_re, table_im, psi_re, psi_im, far_re, far_im))

    partial_value = jnp.zeros((frame_count, length, length), jnp.float32)
    partial_value, stored = lax.scan(
        forward_slot, partial_value, (probe, coefficient[0], coefficient[1], spectrum, wave_index)
    )
    intensity = lax.psum(partial_value, "wave")
    shortfall = jnp.sqrt(measured / jnp.maximum(intensity, floor_level)) - 1.0

    def backward_slot(totals, inputs):
        absorb_coef, phase_coef, weight, table_re, table_im, psi_re, psi_im, far_re, far_im = inputs
        factor = weight * shortfall
        back_re, back_im = transform(
            table_re,
            -table_im,
            (factor * far_re).astype(jnp.bfloat16),
            (factor * far_im).astype(jnp.bfloat16),
        )
        cross_re = psi_re * back_re + psi_im * back_im
        cross_im = psi_re * back_im - psi_im * back_re
        gradient = (
            cross_re[:, None] * (-absorb_coef)[None, :, None, None]
            + cross_im[:, None] * phase_coef[None, :, None, None]
        )
        power_sum = weight * (psi_re * psi_re + psi_im * psi_im)
        return ((totals[0] + gradient, totals[1] + power_sum), None)

    start_totals = (
        jnp.zeros((frame_count, materials, length, length), jnp.float32),
        jnp.zeros((frame_count, length, length), jnp.float32),
    )
    table_re, table_im, psi_re, psi_im, far_re, far_im = stored
    (gradient, power_sum), _ = lax.scan(
        backward_slot,
        start_totals,
        (
            coefficient[0],
            coefficient[1],
            spectrum,
            table_re,
            table_im,
            psi_re,
            psi_im,
            far_re,
            far_im,
        ),
    )
    stacked = jnp.concatenate([gradient, power_sum[:, None]], axis=1)
    accumulated = place_frames(stacked, offsets, columns, margin)
    arrived = padded(edge_cells(accumulated, margin), (("tile", 2),), margin)
    summed = lax.psum(
        fold_rims(accumulated[:, :, margin : margin + columns], arrived, margin), "wave"
    )
    return maps + relax * summed[:materials] / (summed[materials] + 1.0)


def solution(mesh):
    in_specs = (
        P(None, None, "tile"),
        P("tile", None, None),
        P("tile"),
        P("wave", None, None, None),
        P("wave"),
        P("wave"),
        P("wave", None),
        P(),
    )
    out_specs = P(None, None, "tile")
    return jax.shard_map(
        per_device, mesh=mesh, in_specs=in_specs, out_specs=out_specs, check_vma=False
    )
```

profile of v0, /device:TPU:0, one launch (start us, length us, event | category | flops | bytes accessed | tf_op | source)
XLA Modules:
  0.0 355.2 jit_solution(11261539689890777825)
XLA Ops:
  6.5 1.2 fusion.115
  7.7 2.4 collective-permute-start
  10.1 1.3 collective-permute-start.1
  11.4 1.4 fusion.117
  17.3 1.2 pad_maximum_fusion
  18.9 154.0 %while.38 = (s32[]{:T(128)}, f32[2,128,128]{2,1,0:T(8,128)S(1)}, bf16[12,128,128]{2,1,0:T(8,128)(2,1)S(1)}, bf16[12,128,128]{2,1,0:T(8,128)(2,1)S(1)}, f32[12,2,...) while((s32[]{:T(128)}, f32[2,128,128]{2,1,0:T(8,128)S(1)}, ...), condition=%wide.region_1.2_spmd.clone, body=%wide.region_0.1_spmd.clone.sunk | while | flops 71778440 | bytes 5973319 | solution.py:115
  18.9 1.3 fusion.204
  20.2 1.3 fusion.205
  22.7 1.2 bitcast_dynamic-update-slice_fusion.7
  31.7 1.3 fusion.204
  33.0 1.3 fusion.205
  35.5 1.2 bitcast_dynamic-update-slice_fusion.7
  44.5 1.3 fusion.204
  45.9 1.3 fusion.205
  48.3 1.2 bitcast_dynamic-update-slice_fusion.7
  57.3 1.3 fusion.204
  58.7 1.3 fusion.205
  61.2 1.2 bitcast_dynamic-update-slice_fusion.7
  70.2 1.3 fusion.204
  71.5 1.3 fusion.205
  74.0 1.2 bitcast_dynamic-update-slice_fusion.7
  83.0 1.3 fusion.204
  84.4 1.3 fusion.205
  86.8 1.2 bitcast_dynamic-update-slice_fusion.7
  95.8 1.3 fusion.204
  97.2 1.3 fusion.205
  99.7 1.3 bitcast_dynamic-update-slice_fusion.7
  108.7 1.3 fusion.204
  110.1 1.3 fusion.205
  112.5 1.2 bitcast_dynamic-update-slice_fusion.7
  121.5 1.3 fusion.204
  122.9 1.3 fusion.205
  125.3 1.2 bitcast_dynamic-update-slice_fusion.7
  134.3 1.3 fusion.204
  135.7 1.3 fusion.205
  138.2 1.2 bitcast_dynamic-update-slice_fusion.7
  147.2 1.3 fusion.204
  148.6 1.3 fusion.205
  151.0 1.2 bitcast_dynamic-update-slice_fusion.7
  160.0 1.3 fusion.204
  161.4 1.3 fusion.205
  163.9 1.2 bitcast_dynamic-update-slice_fusion.7
  173.6 39.1 %all-reduce.3.cloned.1.call-done = f32[2,128,128]{2,1,0:T(8,128)} async-done(((f32[2,128,128]{2,1,0:T(8,128)}), f32[2,128,128]{2,1,0:T(8,128)}) %all-reduce.3.cloned.1.call-update) | async-done | bytes 131088 | tf_op jit(solution)/shard_map/psum | solution.py:118
  213.7 70.5 %while.39 = (s32[]{:T(128)}, f32[2,4,128,128]{3,2,1,0:T(8,128)S(1)}, f32[2,128,128]{2,1,0:T(8,128)S(1)}, f32[12,2,128,128]{2,3,1,0:T(8,128)}, f32[12]{0:T(128)S(...) while((s32[]{:T(128)}, ...), condition=%wide.region_4.5_spmd.clone, body=%wide.region_3.4_spmd.clone.sunk | while | flops 68583424 | bytes 5898552 | solution.py:144
  214.3 1.6 fusion.229
  220.2 1.6 fusion.229
  226.1 1.6 fusion.229
  232.0 1.6 fusion.229
  237.8 1.6 fusion.229
  243.7 1.6 fusion.229
  249.6 1.6 fusion.229
  255.5 1.6 fusion.229
  261.4 1.6 fusion.229
  267.2 1.6 fusion.229
  273.1 1.6 fusion.229
  279.0 1.6 fusion.229
  284.4 3.1 dynamic_update_slice.44
  287.6 4.5 %dynamic_update_slice.45 = f32[5,128,256]{2,1,0:T(8,128)S(1)} dynamic-update-slice(f32[5,128,256]{2,1,0:T(8,128)S(1)} %dynamic_update_slice.44, f32[5,128,128]{2,1,0:T(8,128)S(1)} %fusion.110, s32[]{:T(128)} %constant.93.clone.1, s32[]{:T(128)} %constant.93.clone.1, s32[]{:T(128)S(6)} %select_n.10) | dynamic-update-slice | bytes 655364 | tf_op jit(solution)/shard_map/dynamic_update_slice | solution.py:77
  292.3 1.3 collective-permute-start.2
  293.6 1.2 collective-permute-done.2
  295.0 1.4 collective-permute-start.3
  296.5 6.6 %collective-permute-done.3 = f32[5,128,64]{2,1,0:T(8,128)S(1)} collective-permute-done((f32[5,128,64]{2,1,0:T(8,128)S(1)}, f32[5,128,64]{2,1,0:T(8,128)S(1)}, u32[]{:S(2)}, u32[]{:S(2)}) %collective-permute-start.3) | collective-permute-done | bytes 163872 | tf_op jit(solution)/shard_map/ppermute | solution.py:20
  304.0 41.8 %all-reduce.5.cloned.1.call-done = f32[5,128,128]{2,1,0:T(8,128)} async-done(((f32[5,128,128]{2,1,0:T(8,128)}), f32[5,128,128]{2,1,0:T(8,128)}) %all-reduce.5.cloned.1.call-update) | async-done | bytes 327696 | tf_op jit(solution)/shard_map/psum | solution.py:162
  346.7 1.7 fusion.112
  (425 shorter events, 155.8 us)
Async XLA Ops:
  6.5 206.2 %all-reduce.3.cloned.1.call-start = ((), (), s32[]{:S(2)}) async-start(), calls=%async_computation | async-start | bytes 262144 | tf_op jit(solution)/shard_map/psum | solution.py:118
  7.7 9.6 %collective-permute-start = (f32[4,128,64]{2,1,0:T(8,128)S(1)}, f32[4,128,64]{2,1,0:T(8,128)S(1)}, u32[]{:S(2)}, u32[]{:S(2)}) collective-permute-start(f32[4,128,64]{2,1,0:T(8,128)S(1)} %get-tuple-element.457), channel_id=1, source_target_pairs={{0,4},{4,8},{8,12},{12,16},{16,20},{20,24},{24,28},{1,5},{5,9},{9,... | collective-permute-start | bytes 393224 | tf_op jit(solution)/shard_map/ppermute | solution.py:17
  10.1 7.3 %collective-permute-start.1 = (f32[4,128,64]{2,1,0:T(8,128)S(1)}, f32[4,128,64]{2,1,0:T(8,128)S(1)}, u32[]{:S(2)}, u32[]{:S(2)}) collective-permute-start(f32[4,128,64]{2,1,0:T(8,128)S(1)} %get-tuple-element.458), channel_id=1, source_target_pairs={{4,0},{8,4},{12,8},{16,12},{20,16},{24,20},{28,24},{5,1},{9,5},{13... | collective-permute-start | bytes 393224 | tf_op jit(solution)/shard_map/ppermute | solution.py:20
  17.3 1.5 copy-start.3
  17.3 1.5 copy-start.4
  18.9 193.9 %copy-start.2 = (f32[2,128,128]{2,1,0:T(8,128)S(1)}, f32[2,128,128]{2,1,0:T(8,128)}, u32[]{:S(2)}) copy-start(f32[2,128,128]{2,1,0:T(8,128)} %param.13) | copy-start | bytes 393220
  172.9 0.7 copy-start
  173.6 172.3 %all-reduce.5.cloned.1.call-start = ((), (), s32[]{:S(2)}) async-start(), calls=%async_computation.1 | async-start | bytes 655360 | tf_op jit(solution)/shard_map/psum | solution.py:162
  292.3 2.5 collective-permute-start.2
  295.0 51.7 %copy-start.1 = (f32[4,128,128]{2,1,0:T(8,128)S(1)}, f32[4,128,128]{2,1,0:T(8,128)}, u32[]{:S(2)}) copy-start(f32[4,128,128]{2,1,0:T(8,128)} %param.12) | copy-start | bytes 786436
  295.0 8.1 %collective-permute-start.3 = (f32[5,128,64]{2,1,0:T(8,128)S(1)}, f32[5,128,64]{2,1,0:T(8,128)S(1)}, u32[]{:S(2)}, u32[]{:S(2)}) collective-permute-start(f32[5,128,64]{2,1,0:T(8,128)S(1)} %get-tuple-element.454), channel_id=1, source_target_pairs={{4,0},{8,4},{12,8},{16,12},{20,16},{24,20},{28,24},{5,1},{9,5},{13... | collective-permute-start | bytes 491528 | tf_op jit(solution)/shard_map/ppermute | solution.py:20
Sparse Core Ops, SparseCore 0:
  173.7 39.0 all-reduce.2
  304.2 41.6 all-reduce.4
where the time goes:
time: 357 us; the launch traced here: 355 us
  matrix products  114 us (32%)
  waiting for transfers between devices  88.8 us (25%)
  local copies, waits for them, and re-layouts  72.2 us (20%)
  other arithmetic  46.8 us (13%)
  between operations  16.3 us (5%)
  loops' own time  10.2 us (3%)
  starting transfers between devices  6.44 us (2%)
    dot_general x96, matrix products, right_product(): jnp.einsum('fkn,nj->fkj', data, table, preferred_element_type=jnp.float32)  53.6 us
    psum x1, waiting for transfers between devices, per_device(): lax.psum(fold_rims(accumulated[:, :, margin:margin + columns], arrived, m...  41.8 us
    psum x1, waiting for transfers between devices, per_device(): intensity = lax.psum(partial_value, 'wave')  39.1 us
    dynamic_slice x72, local copies, waits for them, and re-layouts, per_device(): lax.scan(forward_slot, partial_value, (probe, coefficient[0], coefficient...  36.9 us
    dot_general x96, matrix products, left_product(): jnp.einsum('kn,fnj->fkj', table, data, preferred_element_type=jnp.float32)  29.9 us
    convert_element_type x12, other arithmetic, backward_slot(): (factor * far_im).astype(jnp.bfloat16)  19.7 us
    dynamic_update_slice x24, other arithmetic, per_device(): lax.scan(forward_slot, partial_value, (probe, coefficient[0], coefficient...  19 us
    dot_general x12, matrix products, forward_slot(): jnp.einsum('m,fmrk->frk', absorb_coef, windows, precision=lax.Precision.H...  15 us
  transfers between devices with their start and end apart: 6, of which 4 were waited for; matrix products, arithmetic and copies ran while one was open for 1% of the time, Pallas kernels for 0%

commit v1 on v0

--- a/solution.py
+++ b/solution.py
@@ -159,8 +159,11 @@
     stacked = jnp.concatenate([gradient, power_sum[:, None]], axis=1)
     accumulated = place_frames(stacked, offsets, columns, margin)
     arrived = padded(edge_cells(accumulated, margin), (("tile", 2),), margin)
-    summed = lax.psum(
-        fold_rims(accumulated[:, :, margin : margin + columns], arrived, margin), "wave"
+    summed = jnp.sum(
+        lax.all_gather(
+            fold_rims(accumulated[:, :, margin : margin + columns], arrived, margin), "wave"
+        ),
+        axis=0,
     )
     return maps + relax * summed[:materials] / (summed[materials] + 1.0)
 

time: 357 us -> 353 us (0.989)
    psum x1 -> x0, waiting for transfers between devices: 41.8 us -> none  [per_device(): lax.psum(fold_rims(accumulated[:, :, margin:margin + columns], arrived, m...]
    all_gather x0 -> x1, waiting for transfers between devices: none -> 38.3 us  [per_device(): lax.all_gather(fold_rims(accumulated[:, :, margin:margin + columns], arri...]
where the time goes in v1:
time: 353 us; the launch traced here: 351 us
  matrix products  114 us (32%)
  waiting for transfers between devices  85.3 us (24%)
  local copies, waits for them, and re-layouts  72.2 us (20%)
  other arithmetic  46.4 us (13%)
  between operations  16.4 us (5%)
  loops' own time  10.2 us (3%)
  starting transfers between devices  6.31 us (2%)
    dot_general x96, matrix products, right_product(): jnp.einsum('fkn,nj->fkj', data, table, preferred_element_type=jnp.float32)  53.6 us
    psum x1, waiting for transfers between devices, per_device(): intensity = lax.psum(partial_value, 'wave')  39.1 us
    all_gather x1, waiting for transfers between devices, per_device(): lax.all_gather(fold_rims(accumulated[:, :, margin:margin + columns], arri...  38.3 us
    dynamic_slice x72, local copies, waits for them, and re-layouts, per_device(): lax.scan(forward_slot, partial_value, (probe, coefficient[0], coefficient...  36.9 us
    dot_general x96, matrix products, left_product(): jnp.einsum('kn,fnj->fkj', table, data, preferred_element_type=jnp.float32)  29.9 us
    convert_element_type x12, other arithmetic, backward_slot(): (factor * far_im).astype(jnp.bfloat16)  19.7 us
    dynamic_update_slice x24, other arithmetic, per_device(): lax.scan(forward_slot, partial_value, (probe, coefficient[0], coefficient...  19 us
    dot_general x12, matrix products, forward_slot(): jnp.einsum('m,fmrk->frk', absorb_coef, windows, precision=lax.Precision.H...  15 us
  transfers between devices with their start and end apart: 6, of which 4 were waited for; matrix products, arithmetic and copies ran while one was open for 1% of the time, Pallas kernels for 0%

profile of v1, /device:TPU:0, one launch (start us, length us, event | category | flops | bytes accessed | tf_op | source)
XLA Modules:
  0.0 351.2 jit_solution(1813766870148725541)
XLA Ops:
  6.5 1.2 fusion.115
  7.7 2.4 collective-permute-start
  10.1 1.3 collective-permute-start.1
  11.4 1.4 fusion.117
  17.3 1.2 pad_maximum_fusion
  18.9 154.0 %while.38 = (s32[]{:T(128)}, f32[2,128,128]{2,1,0:T(8,128)S(1)}, bf16[12,128,128]{2,1,0:T(8,128)(2,1)S(1)}, bf16[12,128,128]{2,1,0:T(8,128)(2,1)S(1)}, f32[12,2,...) while((s32[]{:T(128)}, f32[2,128,128]{2,1,0:T(8,128)S(1)}, ...), condition=%wide.region_1.2_spmd.clone, body=%wide.region_0.1_spmd.clone.sunk | while | flops 71778440 | bytes 5973319 | solution.py:115
  18.9 1.3 fusion.204
  20.2 1.3 fusion.205
  22.7 1.2 bitcast_dynamic-update-slice_fusion.7
  31.7 1.3 fusion.204
  33.0 1.3 fusion.205
  35.5 1.2 bitcast_dynamic-update-slice_fusion.7
  44.5 1.3 fusion.204
  45.9 1.3 fusion.205
  48.3 1.2 bitcast_dynamic-update-slice_fusion.7
  57.3 1.3 fusion.204
  58.7 1.3 fusion.205
  61.2 1.2 bitcast_dynamic-update-slice_fusion.7
  70.2 1.3 fusion.204
  71.5 1.3 fusion.205
  74.0 1.2 bitcast_dynamic-update-slice_fusion.7
  83.0 1.3 fusion.204
  84.4 1.3 fusion.205
  86.8 1.2 bitcast_dynamic-update-slice_fusion.7
  95.8 1.3 fusion.204
  97.2 1.3 fusion.205
  99.7 1.3 bitcast_dynamic-update-slice_fusion.7
  108.7 1.3 fusion.204
  110.1 1.3 fusion.205
  112.5 1.2 bitcast_dynamic-update-slice_fusion.7
  121.5 1.3 fusion.204
  122.9 1.3 fusion.205
  125.3 1.2 bitcast_dynamic-update-slice_fusion.7
  134.3 1.3 fusion.204
  135.7 1.3 fusion.205
  138.2 1.2 bitcast_dynamic-update-slice_fusion.7
  147.2 1.3 fusion.204
  148.6 1.3 fusion.205
  151.0 1.2 bitcast_dynamic-update-slice_fusion.7
  160.0 1.3 fusion.204
  161.4 1.3 fusion.205
  163.9 1.2 bitcast_dynamic-update-slice_fusion.7
  173.6 39.1 %all-reduce.2.cloned.1.call-done = f32[2,128,128]{2,1,0:T(8,128)} async-done(((f32[2,128,128]{2,1,0:T(8,128)}), f32[2,128,128]{2,1,0:T(8,128)}) %all-reduce.2.cloned.1.call-update) | async-done | bytes 131088 | tf_op jit(solution)/shard_map/psum | solution.py:118
  213.7 70.5 %while.39 = (s32[]{:T(128)}, f32[2,4,128,128]{3,2,1,0:T(8,128)S(1)}, f32[2,128,128]{2,1,0:T(8,128)S(1)}, f32[12,2,128,128]{2,3,1,0:T(8,128)}, f32[12]{0:T(128)S(...) while((s32[]{:T(128)}, ...), condition=%wide.region_4.5_spmd.clone, body=%wide.region_3.4_spmd.clone.sunk | while | flops 68583424 | bytes 5898552 | solution.py:144
  214.3 1.6 fusion.229
  220.2 1.6 fusion.229
  226.1 1.6 fusion.229
  232.0 1.6 fusion.229
  237.8 1.6 fusion.229
  243.7 1.6 fusion.229
  249.6 1.6 fusion.229
  255.5 1.6 fusion.229
  261.4 1.6 fusion.229
  267.2 1.6 fusion.229
  273.1 1.6 fusion.229
  279.0 1.6 fusion.229
  284.4 3.1 dynamic_update_slice.44
  287.6 4.5 %dynamic_update_slice.45 = f32[5,128,256]{2,1,0:T(8,128)S(1)} dynamic-update-slice(f32[5,128,256]{2,1,0:T(8,128)S(1)} %dynamic_update_slice.44, f32[5,128,128]{2,1,0:T(8,128)S(1)} %fusion.110, s32[]{:T(128)} %constant.94.clone.1, s32[]{:T(128)} %constant.94.clone.1, s32[]{:T(128)S(6)} %select_n.10) | dynamic-update-slice | bytes 655364 | tf_op jit(solution)/shard_map/dynamic_update_slice | solution.py:77
  292.3 1.3 collective-permute-start.2
  293.6 1.2 collective-permute-done.2
  295.0 1.3 collective-permute-start.3
  296.3 6.6 %collective-permute-done.3 = f32[5,128,64]{2,1,0:T(8,128)S(1)} collective-permute-done((f32[5,128,64]{2,1,0:T(8,128)S(1)}, f32[5,128,64]{2,1,0:T(8,128)S(1)}, u32[]{:S(2)}, u32[]{:S(2)}) %collective-permute-start.3) | collective-permute-done | bytes 163872 | tf_op jit(solution)/shard_map/ppermute | solution.py:20
  303.9 38.3 %all-gather.3.cloned.1.call-done = f32[20,128,128]{2,1,0:T(8,128)} async-done(((f32[5,128,128]{2,1,0:T(8,128)}), f32[20,128,128]{2,1,0:T(8,128)}) %all-gather.3.cloned.1.call-update) | async-done | bytes 1310736 | tf_op jit(solution)/shard_map/all_gather | solution.py:163
  342.2 1.4 reduce_sum.9
  (426 shorter events, 155.7 us)
Async XLA Ops:
  6.5 206.2 %all-reduce.2.cloned.1.call-start = ((), (), s32[]{:S(2)}) async-start(), calls=%async_computation | async-start | bytes 262144 | tf_op jit(solution)/shard_map/psum | solution.py:118
  7.7 9.6 %collective-permute-start = (f32[4,128,64]{2,1,0:T(8,128)S(1)}, f32[4,128,64]{2,1,0:T(8,128)S(1)}, u32[]{:S(2)}, u32[]{:S(2)}) collective-permute-start(f32[4,128,64]{2,1,0:T(8,128)S(1)} %get-tuple-element.484), channel_id=1, source_target_pairs={{0,4},{4,8},{8,12},{12,16},{16,20},{20,24},{24,28},{1,5},{5,9},{9,... | collective-permute-start | bytes 393224 | tf_op jit(solution)/shard_map/ppermute | solution.py:17
  10.1 7.3 %collective-permute-start.1 = (f32[4,128,64]{2,1,0:T(8,128)S(1)}, f32[4,128,64]{2,1,0:T(8,128)S(1)}, u32[]{:S(2)}, u32[]{:S(2)}) collective-permute-start(f32[4,128,64]{2,1,0:T(8,128)S(1)} %get-tuple-element.485), channel_id=1, source_target_pairs={{4,0},{8,4},{12,8},{16,12},{20,16},{24,20},{28,24},{5,1},{9,5},{13... | collective-permute-start | bytes 393224 | tf_op jit(solution)/shard_map/ppermute | solution.py:20
  17.3 1.5 copy-start.3
  17.3 1.5 copy-start.4
  18.9 193.9 %copy-start.2 = (f32[2,128,128]{2,1,0:T(8,128)S(1)}, f32[2,128,128]{2,1,0:T(8,128)}, u32[]{:S(2)}) copy-start(f32[2,128,128]{2,1,0:T(8,128)} %param.13) | copy-start | bytes 393220
  172.9 0.7 copy-start
  173.6 168.7 %all-gather.3.cloned.1.call-start = ((), (), s32[]{:S(2)}) async-start(), calls=%async_computation.1 | async-start | bytes 1638400 | tf_op jit(solution)/shard_map/all_gather | solution.py:163
  292.3 2.5 collective-permute-start.2
  295.0 7.9 %collective-permute-start.3 = (f32[5,128,64]{2,1,0:T(8,128)S(1)}, f32[5,128,64]{2,1,0:T(8,128)S(1)}, u32[]{:S(2)}, u32[]{:S(2)}) collective-permute-start(f32[5,128,64]{2,1,0:T(8,128)S(1)} %get-tuple-element.481), channel_id=1, source_target_pairs={{4,0},{8,4},{12,8},{16,12},{20,16},{24,20},{28,24},{5,1},{9,5},{13... | collective-permute-start | bytes 491528 | tf_op jit(solution)/shard_map/ppermute | solution.py:20
  303.0 40.7 %copy-start.1 = (f32[4,128,128]{2,1,0:T(8,128)S(1)}, f32[4,128,128]{2,1,0:T(8,128)}, u32[]{:S(2)}) copy-start(f32[4,128,128]{2,1,0:T(8,128)} %param.12) | copy-start | bytes 786436
Sparse Core Ops, SparseCore 0:
  173.7 39.0 all-reduce.1
  304.0 38.1 all-gather.2
